TPU v7x, 256 devices: a whole 4x4x8 slice. The times are simulated.
256 devices in a mesh: ep: 32 (over y, x, core), dp: 8 (over z).
Axes of the slice: x: 4, y: 4, z: 8, core: 2. Of those that a mesh axis runs over, the one named last changes fastest.
Arguments:
- out_grad: bfloat16 [8, 4096, 2048], P('dp', 'ep'), may hold values from -6 to 6
- gates: bfloat16 [8, 4096, 8], P('dp', 'ep'), may hold values from 0.019897461 to 0.5
- routes: int32 [8, 4096, 8], P('dp', 'ep'), may hold values from 0 to 127, all different within a row; in each aligned block of 128 rows (0 to 127, 128 to 255, ..., all dimensions but the last counted through in order) at most 12 rows name the same one
- expert_slot: int32 [128], replicated, may hold values from 0 to 127, each once
- hidden_saved: bfloat16 [8, 128, 32, 12, 768], P('dp', 'ep'), may hold values from -6 to 6
- w_down: bfloat16 [2048, 98304], P('dp', 'ep'), may hold values from -0.21875 to 0.21875
Outputs:
- hidden_grad: bfloat16 [8, 128, 32, 12, 768], P('dp', 'ep')
- gate_grad: float32 [8, 4096, 8], P('dp', 'ep')
- weight_grad: float32 [2048, 98304], P('dp', 'ep')
Inputs may be any that keep to these rules, and one draw needn't show every extreme that they name: `routes`: the rows of one device name no expert more than 12 times, and every expert is named by some row. `expert_slot`: each slot once.
All inputs are finite; a program needn't handle non-finite values.
Results may differ from a plain program's by a relative error of at most 0.012.
Values may be sent and summed in bfloat16 or wider, within the bound.
A program may use at most 128 MiB of HBM per device.

v0:
```python
import jax
import jax.numpy as jnp
from jax import lax
from jax.sharding import PartitionSpec as P


def local(out_grad, gates, routes, expert_slot, hidden_saved, w_down):
    tokens = out_grad.shape[1]
    width = out_grad.shape[2]
    chosen = routes.shape[2]
    experts = expert_slot.shape[0]
    n_ep = lax.axis_size("ep")
    exp_dev = experts // n_ep
    slots = hidden_saved.shape[3]
    hidden = hidden_saved.shape[4]
    flat_ids = routes.reshape(-1)
    onehot = (flat_ids[:, None] == jnp.arange(experts, dtype=jnp.int32)[None, :]).astype(jnp.int32)
    slot_ids = jnp.sum(onehot * expert_slot[None, :], axis=1)
    ranks = jnp.sum(onehot * (jnp.cumsum(onehot, axis=0) - 1), axis=1)
    target = slot_ids * slots + ranks
    rows = jnp.repeat(out_grad[0], chosen, axis=0)
    send_rows = jnp.zeros((experts * slots, width), jnp.bfloat16).at[target].set(rows)
    send_gates = jnp.zeros((experts * slots,), jnp.bfloat16).at[target].set(gates.reshape(-1))
    recv_rows, recv_gates = (
        lax.all_to_all(
            send_rows.reshape(n_ep, exp_dev * slots, width),
            "ep",
            split_axis=0,
            concat_axis=0,
            tiled=True,
        ),
        lax.all_to_all(
            send_gates.reshape(n_ep, exp_dev * slots), "ep", split_axis=0, concat_axis=0, tiled=True
        ),
    )
    recv_rows = recv_rows.reshape(n_ep, exp_dev, slots, width)
    saved = hidden_saved[0]
    w_all = lax.all_gather(w_down, "dp", axis=0, tiled=True).reshape(width, exp_dev, hidden)
    upstream = jnp.einsum("slcd,dlj->lscj", recv_rows, w_all, preferred_element_type=jnp.float32)
    gates_lsc = recv_gates.reshape(n_ep, exp_dev, slots).transpose(1, 0, 2).astype(jnp.float32)
    hidden_grad = (gates_lsc[..., None] * upstream).astype(jnp.bfloat16)[None]
    slot_grad = jnp.sum(saved.astype(jnp.float32) * upstream, axis=3)
    returned = lax.all_to_all(
        slot_grad.transpose(1, 0, 2).reshape(n_ep, exp_dev * slots),
        "ep",
        split_axis=0,
        concat_axis=0,
        tiled=True,
    )
    gate_grad = returned.reshape(-1)[target].reshape(1, tokens, chosen)
    scaled = (gates_lsc[..., None] * saved.astype(jnp.float32)).astype(jnp.bfloat16)
    term = jnp.einsum("slcd,lscj->dlj", recv_rows, scaled, preferred_element_type=jnp.float32)
    weight_grad = lax.psum_scatter(
        term.reshape(width // lax.axis_size("dp") * lax.axis_size("dp"), exp_dev * hidden).astype(
            jnp.bfloat16
        ),
        "dp",
        scatter_dimension=0,
        tiled=True,
    ).astype(jnp.float32)
    return (hidden_grad, gate_grad, weight_grad)


def solution(mesh):
    return jax.shard_map(
        local,
        mesh=mesh,
        in_specs=(
            P("dp", "ep", None),
            P("dp", "ep", None),
            P("dp", "ep", None),
            P(),
            P("dp", "ep", None, None, None),
            P("dp", "ep"),
        ),
        out_specs=(P("dp", "ep", None, None, None), P("dp", "ep", None), P("dp", "ep")),
        check_vma=False,
    )
```

profile of v0, /device:TPU:33, one launch (start us, length us, event | category | flops | bytes accessed | tf_op | source)
XLA Modules:
  0.0 297.3 jit_solution(12767671879076175507)
XLA Ops:
  7.3 2.6 copy.55
  10.2 0.1 copy.50
  10.3 0.1 reshape.113
  10.5 0.2 fusion.11
  11.0 0.5 select_reduce_fusion
  11.5 7.6 %scatter_custom_fusion = bf16[1536]{0:T(1024)(128)(2,1)S(1)} fusion(s32[1024]{0:T(1024)S(1)} %bitcast.56, bf16[1024]{0:T(1024)(128)(2,1)S(1)} %reshape.113, bf16[]{:T(256)} %constant.6.clone.1), kind=kCustom, calls=%fused_computation.30 | custom fusion | bytes 3074 | tf_op jit(solution)/shard_map/scatter | solution.py:23
  19.1 0.7 all_to_all.20
  19.8 7.8 %all-to-all-start = ((bf16[32,1,48]{2,1,0:T(2,128)(2,1)}), bf16[32,1,48]{2,1,0:T(2,128)(2,1)S(1)}, u32[]{:S(2)}, u32[]{:S(2)}) async-start(bf16[32,1,48]{2,1,0:T(2,128)(2,1)} %all_to_all.20), calls=%async_computation | async-start | bytes 32768 | tf_op jit(solution)/shard_map/all_to_all | solution.py:32
  27.6 10.1 %scatter_custom_fusion.1 = bf16[1536,2048]{1,0:T(8,128)(2,1)} fusion(s32[1024]{0:T(1024)S(1)} %bitcast.57, bf16[]{:T(256)} %constant.6.clone.1, bf16[128,2048]{1,0:T(8,128)(2,1)S(1)} %bitcast.47), kind=kCustom, calls=%fused_computation.9 | custom fusion | bytes 6815746 | tf_op jit(solution)/shard_map/scatter | solution.py:22
  37.7 7.6 %all-to-all-start.1 = ((bf16[32,48,2048]{2,1,0:T(8,128)(2,1)}), bf16[32,48,2048]{2,1,0:T(8,128)(2,1)}, u32[]{:S(2)}, u32[]{:S(2)}) async-start(bf16[32,48,2048]{2,1,0:T(8,128)(2,1)} %bitcast.48), calls=%async_computation.1 | async-start | bytes 12582912 | tf_op jit(solution)/shard_map/all_to_all | solution.py:25
  45.5 72.8 %all-to-all-done.1 = bf16[32,48,2048]{2,1,0:T(8,128)(2,1)} async-done(((bf16[32,48,2048]{2,1,0:T(8,128)(2,1)}), bf16[32,48,2048]{2,1,0:T(8,128)(2,1)}, u32[]{:S(2)}, u32[]{:S(2)}) %all-to-all-start.1) | async-done | bytes 6291488 | tf_op jit(solution)/shard_map/all_to_all | solution.py:25
  118.3 6.3 %copy.54 = bf16[32,48,2048]{2,0,1:T(8,128)(2,1)S(1)} copy(bf16[32,48,2048]{2,1,0:T(8,128)(2,1)} %all-to-all-done.1) | data formatting | bytes 12582912 | tf_op jit(solution)/shard_map/all_to_all | solution.py:25
  124.6 9.9 %bitcast_convert_fusion = bf16[4,768,2048]{2,1,0:T(8,128)(2,1)} fusion(bf16[32,4,12,2048]{3,0,2,1:T(8,128)(2,1)S(1)} %bitcast.50, bf16[1,4,32,12,768]{4,2,3,1,0:T(8,128)(2,1)S(1)} %copy-done.6, f32[4,32,12]{1,2,0:T(8,128)S(1)} %bitcast.52), kind=kOutput, calls=%fused_computation.3 | convolution fusion | flops 4841668608 | bytes 21239808 | tf_op jit(solution)/shard_map/slcd,lscj->dlj/dot_general | solution.py:52
  134.5 16.7 %copy.58 = bf16[2048,3072]{1,0:T(8,128)(2,1)} copy(bf16[2048,3072]{0,1:T(8,128)(2,1)} %bitcast.49) | data formatting | bytes 25165824 | tf_op jit(solution)/shard_map/convert_element_type | solution.py:54
  151.3 15.5 %fusion = (f32[4,32,12]{1,2,0:T(8,128)S(1)}, bf16[1,4,32,12,768]{4,2,3,1,0:T(8,128)(2,1)}) fusion(bf16[1,4,32,12,768]{4,2,3,1,0:T(8,128)(2,1)S(1)} %copy-done.6, f32[4,32,12]{1,2,0:T(8,128)S(1)} %bitcast.53, bf16[32,4,12,2048]{3,0,2,1:T(8,128)(2,1)} %bitcast.51, bf16[2048,4,768,1]{0,2,3,1:T(8,128)(2,1)} %bitcast.59), kind=kOutput, calls=%fused_computation.6 | convolution fusion | flops 4837734912 | bytes 23605248 | tf_op jit(solution)/shard_map/slcd,dlj->lscj/dot_general | solution.py:39
  166.9 0.7 copy.57
  167.5 8.7 %all-to-all-start.2 = ((f32[32,1,48]{2,1,0:T(1,128)}), f32[32,1,48]{2,1,0:T(1,128)S(1)}, u32[]{:S(2)}, u32[]{:S(2)}) async-start(f32[32,1,48]{2,1,0:T(1,128)} %copy.57), calls=%async_computation.2 | async-start | bytes 32768 | tf_op jit(solution)/shard_map/all_to_all | solution.py:43
  176.3 7.0 %all-to-all-done.2 = f32[32,1,48]{2,1,0:T(1,128)S(1)} async-done(((f32[32,1,48]{2,1,0:T(1,128)}), f32[32,1,48]{2,1,0:T(1,128)S(1)}, u32[]{:S(2)}, u32[]{:S(2)}) %all-to-all-start.2) | async-done | bytes 6176 | tf_op jit(solution)/shard_map/all_to_all | solution.py:43
  183.2 0.5 broadcast.71
  183.7 0.7 reduce.3
  184.5 6.1 %gather_fusion = f32[1024]{0:T(1024)S(1)} fusion(f32[1536]{0:T(1024)S(1)} %reshape.97, s32[1024]{0:T(1024)S(1)} %broadcast_clamp_fusion), kind=kCustom, calls=%fused_computation | custom fusion | bytes 12288 | tf_op jit(solution)/shard_map/gather | solution.py:50
  190.7 0.7 copy.59
  191.4 95.6 %reduce-scatter.2.cloned.1.call-done = bf16[256,3072]{1,0:T(8,128)(2,1)} async-done(((bf16[2048,3072]{1,0:T(8,128)(2,1)}), bf16[256,3072]{1,0:T(8,128)(2,1)}) %reduce-scatter.2.cloned.1.call-update) | async-done | bytes 1572880 | tf_op jit(solution)/shard_map/reduce_scatter | solution.py:53
  287.0 3.4 %convert_element_type.50 = f32[256,3072]{1,0:T(8,128)} convert(bf16[256,3072]{1,0:T(8,128)(2,1)} %reduce-scatter.2.cloned.1.call-done) | non-fusion elementwise | flops 786432 | bytes 4718592 | tf_op jit(solution)/shard_map/convert_element_type | solution.py:60
  (38 shorter events, 1.0 us)
Async XLA Ops:
  7.2 20.4 %copy-start = (bf16[1,128,2048]{2,1,0:T(8,128)(2,1)S(1)}, bf16[1,128,2048]{2,1,0:T(8,128)(2,1)}, u32[]{:S(2)}) copy-start(bf16[1,128,2048]{2,1,0:T(8,128)(2,1)} %param.6) | copy-start | bytes 1572868
  7.2 2.7 copy-start.3
  7.2 3.0 %copy-start.4 = (bf16[1,128,8]{1,2,0:T(8,128)(2,1)S(1)}, bf16[1,128,8]{1,2,0:T(8,128)(2,1)}, u32[]{:S(2)}) copy-start(bf16[1,128,8]{1,2,0:T(8,128)(2,1)} %param.7) | copy-start | bytes 6148
  7.2 3.8 %copy-start.5 = (s32[128]{0:T(128)S(1)}, s32[128]{0:T(128)}, u32[]{:S(2)}) copy-start(s32[128]{0:T(128)} %param.9) | copy-start | bytes 1540
  7.2 144.1 %all-gather.2.cloned.1.call-start = ((), (), s32[]{:S(2)}) async-start(), calls=%async_computation.4 | async-start | bytes 14155776 | tf_op jit(solution)/shard_map/all_gather | solution.py:38
  19.8 17.9 %all-to-all-start = ((bf16[32,1,48]{2,1,0:T(2,128)(2,1)}), bf16[32,1,48]{2,1,0:T(2,128)(2,1)S(1)}, u32[]{:S(2)}, u32[]{:S(2)}) async-start(bf16[32,1,48]{2,1,0:T(2,128)(2,1)} %all_to_all.20), calls=%async_computation | async-start | bytes 32768 | tf_op jit(solution)/shard_map/all_to_all | solution.py:32
  37.7 80.6 %all-to-all-start.1 = ((bf16[32,48,2048]{2,1,0:T(8,128)(2,1)}), bf16[32,48,2048]{2,1,0:T(8,128)(2,1)}, u32[]{:S(2)}, u32[]{:S(2)}) async-start(bf16[32,48,2048]{2,1,0:T(8,128)(2,1)} %bitcast.48), calls=%async_computation.1 | async-start | bytes 12582912 | tf_op jit(solution)/shard_map/all_to_all | solution.py:25
  45.3 241.7 %reduce-scatter.2.cloned.1.call-start = ((), (), s32[]{:S(2)}) async-start(), calls=%async_computation.5 | async-start | bytes 14155776 | tf_op jit(solution)/shard_map/reduce_scatter | solution.py:53
  45.5 79.2 %copy-start.6 = (bf16[1,4,32,12,768]{4,2,3,1,0:T(8,128)(2,1)S(1)}, bf16[1,4,32,12,768]{4,2,3,1,0:T(8,128)(2,1)}, u32[]{:S(2)}) copy-start(bf16[1,4,32,12,768]{4,2,3,1,0:T(8,128)(2,1)} %param.10) | copy-start | bytes 7077892
  124.6 9.9 %copy-start.2 = (bf16[32,48,2048]{2,0,1:T(8,128)(2,1)}, bf16[32,48,2048]{2,0,1:T(8,128)(2,1)S(1)}, u32[]{:S(2)}) copy-start(bf16[32,48,2048]{2,0,1:T(8,128)(2,1)S(1)} %copy.54) | copy-start | bytes 18874372
  151.3 139.2 %copy-start.1 = (bf16[1,128,2048]{2,1,0:T(8,128)(2,1)S(1)}, bf16[1,128,2048]{2,1,0:T(8,128)(2,1)}, u32[]{:S(2)}) copy-start(bf16[1,128,2048]{2,1,0:T(8,128)(2,1)} %param.6) | copy-start | bytes 1572868
  167.5 15.7 %all-to-all-start.2 = ((f32[32,1,48]{2,1,0:T(1,128)}), f32[32,1,48]{2,1,0:T(1,128)S(1)}, u32[]{:S(2)}, u32[]{:S(2)}) async-start(f32[32,1,48]{2,1,0:T(1,128)} %copy.57), calls=%async_computation.2 | async-start | bytes 32768 | tf_op jit(solution)/shard_map/all_to_all | solution.py:43
Sparse Core Ops, SparseCore 0:
  10.3 139.5 all-gather.1
  152.5 134.4 reduce-scatter.1
where the time goes:
time: 301 us; the launch traced here: 297 us
  waiting for transfers between devices  175 us (58%)
  local copies, waits for them, and re-layouts  53.1 us (18%)
  matrix products  25.4 us (8%)
  starting transfers between devices  24.1 us (8%)
  between operations  14.3 us (5%)
  other arithmetic  4.91 us (2%)
    reduce_scatter x1, waiting for transfers between devices, local(): lax.psum_scatter(term.reshape(width // lax.axis_size('dp') * lax.axis_siz...  95.6 us
    all_to_all x1, waiting for transfers between devices, local(): lax.all_to_all(send_rows.reshape(n_ep, exp_dev * slots, width), 'ep', spl...  72.8 us
    convert_element_type x1, local copies, waits for them, and re-layouts, local(): term.reshape(width // lax.axis_size('dp') * lax.axis_size('dp'), exp_dev...  16.7 us
    dot_general x1, matrix products, local(): jnp.einsum('slcd,dlj->lscj', recv_rows, w_all, preferred_element_type=jnp...  15.5 us
    scatter x1, local copies, waits for them, and re-layouts, local(): jnp.zeros((experts * slots, width), jnp.bfloat16).at[target].set(rows)  10.1 us
    dot_general x1, matrix products, local(): jnp.einsum('slcd,lscj->dlj', recv_rows, scaled, preferred_element_type=jn...  9.89 us
    all_to_all x1, starting transfers between devices, local(): lax.all_to_all(slot_grad.transpose(1, 0, 2).reshape(n_ep, exp_dev * slots...  8.69 us
    all_to_all x1, starting transfers between devices, local(): lax.all_to_all(send_gates.reshape(n_ep, exp_dev * slots), 'ep', split_axi...  7.76 us
  transfers between devices with their start and end apart: 5, of which 3 were waited for; matrix products, arithmetic and copies ran while one was open for 26% of the time, Pallas kernels for 0%

commit v1 on v0

v1 whole, which is shorter than its diff:
```python
import jax
import jax.numpy as jnp
from jax import lax
from jax.experimental import pallas as pl
from jax.experimental.pallas import tpu as pltpu
from jax.sharding import PartitionSpec as P

BF = jnp.bfloat16
F32 = jnp.float32
MESH = pl.DeviceIdType.MESH
NX, NY, NC, NZ = 4, 4, 2, 8
NE = NX * NY * NC
TOK, D, TOPK = 128, 2048, 8
EXPERTS, LOCAL, CAP, HID = 128, 4, 12, 768
DS = D // NZ
EXT = D + 2 * EXPERTS
ROWS = CAP * NE
SUB = DS // 4
STEPS = NZ - 1


def kernel(
    w_ref, og_ref, rt_ref, gt_ref, es_ref, hs_ref,
    hg_ref, gg_ref, wg_ref,
    T, W, X, G, S, H, R, Fst, Tm, SG, O, Pb, meta,
    ag_s, ag_r, rs_s, rs_r, tk_s, tk_r, sg_s, sg_r, loc,
):
    ep, z = lax.axis_index("ep"), lax.axis_index("dp")
    c, x, y = ep % NC, (ep // NC) % NX, ep // (NC * NX)

    def at(yy, xx, cc):
        return ((yy * NX + xx) * NC + cc, z)

    x_up, x_dn = (x + 1) % NX, (x + NX - 1) % NX
    y_up, y_dn = (y + 1) % NY, (y + NY - 1) % NY
    z_up, z_dn = (ep, (z + 1) % NZ), (ep, (z + NZ - 1) % NZ)
    to_xu, to_xd, to_yu, to_yd = at(y, x_up, c), at(y, x_dn, c), at(y_up, x, c), at(y_dn, x, c)
    sibling = at(y, x, 1 - c)

    barrier = pltpu.get_barrier_semaphore()
    for other in (z_up, z_dn, to_xu, to_xd, to_yu, to_yd, sibling):
        pl.semaphore_signal(barrier, inc=1, device_id=other, device_id_type=MESH)
    pl.semaphore_wait(barrier, 7)

    def ag(t, i):
        rows = pl.ds(i * SUB, SUB)
        owner = (z + NZ - t) % NZ if i < 2 else (z + t) % NZ
        return pltpu.make_async_remote_copy(
            src_ref=w_ref.at[rows] if t == 0 else W.at[owner, rows],
            dst_ref=W.at[owner, rows],
            send_sem=ag_s.at[t, i],
            recv_sem=ag_r.at[t, i],
            device_id=z_up if i < 2 else z_dn,
            device_id_type=MESH,
        )

    def ag_next(t, streams):
        for i in streams:
            ag(t, i).wait_recv()
            ag(t + 1, i).start()

    for i in (0, 2, 1, 3):
        ag(0, i).start()
    own_tokens = pltpu.make_async_copy(og_ref, T.at[c, y, x, :, pl.ds(0, D)], loc.at[0])
    own_tokens.start()
    own_saved = pltpu.make_async_copy(hs_ref, H, loc.at[1])
    own_saved.start()
    own_w = pltpu.make_async_copy(w_ref, W.at[z], loc.at[2])
    own_w.start()

    io0 = lax.broadcasted_iota(jnp.int32, (EXPERTS, TOK), 0)
    io1 = lax.broadcasted_iota(jnp.int32, (EXPERTS, TOK), 1)
    es = es_ref[...]
    to_slot = (io0 == es).astype(F32).astype(BF)
    slot_of = jnp.transpose(jnp.broadcast_to(es.astype(F32), (EXPERTS, EXPERTS)))
    named = jnp.zeros((EXPERTS, TOK), F32)
    weight = jnp.zeros((EXPERTS, TOK), F32)
    for k in range(TOPK):
        hit = (io0 == rt_ref[k : k + 1, :]).astype(F32)
        named = named + hit
        weight = weight + hit * gt_ref[k : k + 1, :].astype(F32)
        meta[k : k + 1, :] = jnp.sum(hit * slot_of, axis=0, keepdims=True)
    earlier = (io0 < io1).astype(F32).astype(BF)
    rank = jnp.dot(named.astype(BF), earlier, preferred_element_type=F32)
    for k in range(TOPK):
        hit = (io0 == rt_ref[k : k + 1, :]).astype(F32)
        meta[TOPK + k : TOPK + k + 1, :] = jnp.sum(hit * rank, axis=0, keepdims=True)
    ranks = jnp.dot(to_slot, ((rank + 1.0) * named).astype(BF), preferred_element_type=F32)
    gates = jnp.dot(to_slot, weight.astype(BF), preferred_element_type=F32)
    T[c, y, x, :, D : D + EXPERTS] = ranks.astype(BF)
    T[c, y, x, :, D + EXPERTS : EXT] = jnp.transpose(gates).astype(BF)
    own_tokens.wait()

    half = TOK // 2
    up_rows, dn_rows = pl.ds(0, half), pl.ds(half, half)
    quarter = [pl.ds(i * half // 2, half // 2) for i in range(4)]

    def tk(n, ref, other):
        return pltpu.make_async_remote_copy(
            src_ref=ref,
            dst_ref=ref,
            send_sem=tk_s.at[n],
            recv_sem=tk_r.at[n],
            device_id=other,
            device_id_type=MESH,
        )

    every = pl.ds(0, 4)
    tokens = [
        [
            tk(0, T.at[c, y, x, up_rows], to_xu),
            tk(1, T.at[c, y, x, up_rows], to_xd),
            tk(2, T.at[c, y, x, dn_rows], to_yu),
            tk(3, T.at[c, y, x, dn_rows], to_yd),
        ],
        [
            tk(4, T.at[c, y, x_dn, quarter[0]], to_xu),
            tk(5, T.at[c, y, x_up, quarter[1]], to_xd),
            tk(6, T.at[c, y_dn, x, quarter[2]], to_yu),
            tk(7, T.at[c, y_up, x, quarter[3]], to_yd),
        ],
        [
            tk(8, T.at[c, y, every, up_rows], to_yu),
            tk(9, T.at[c, y, every, up_rows], to_yd),
            tk(10, T.at[c, every, x, dn_rows], to_xu),
            tk(11, T.at[c, every, x, dn_rows], to_xd),
        ],
        [
            tk(12, T.at[c, y_dn, every, quarter[0]], to_yu),
            tk(13, T.at[c, y_up, every, quarter[1]], to_yd),
            tk(14, T.at[c, every, x_dn, quarter[2]], to_xu),
            tk(15, T.at[c, every, x_up, quarter[3]], to_xd),
        ],
        [tk(16, T.at[c, pl.ds(0, 2)], sibling), tk(17, T.at[c, pl.ds(2, 2)], sibling)],
    ]

    def phase(n):
        if n > 0:
            for copy in tokens[n - 1]:
                copy.wait_recv()
        for copy in tokens[n]:
            copy.start()

    phase(0)
    ag_next(0, (0, 2))
    phase(1)
    ag_next(0, (1, 3))
    phase(2)
    ag_next(1, (0, 2))
    ag_next(1, (1, 3))
    ag_next(2, (0, 2))
    phase(3)
    ag_next(2, (1, 3))
    ag_next(3, (0, 2))
    phase(4)
    ag_next(3, (1, 3))
    ag_next(4, (0, 2))
    own_saved.wait()
    tokens[4][0].wait_recv()
    ag_next(4, (1, 3))

    group = ROWS // 2
    io_row = lax.broadcasted_iota(jnp.int32, (group, TOK), 0).astype(F32)
    io16 = lax.broadcasted_iota(jnp.int32, (16, TOK), 0)
    first = pl.multiple_of((ep // 4) * 16, 16)
    wide = 256

    def unit(u, carry):
        a, l = u // LOCAL, u % LOCAL

        @pl.when(u == 2)
        def _():
            ag_next(5, (0, 2))

        @pl.when(u == 4)
        def _():
            tokens[4][1].wait_recv()
            ag_next(5, (1, 3))

        for block in range(16):
            cc, yy, xx = block // 8, (block // 4) % 2, block % 4
            sixteen = T[cc, 2 * a + yy, xx, pl.ds(first, 16), D : D + EXPERTS].astype(F32)
            v = jnp.sum(
                jnp.where(io16 == (ep % 4) * 4 + l, sixteen, 0.0), axis=0, keepdims=True
            )
            source = (yy * NX + xx) * NC + cc
            v = jnp.where(v > 0.5, 16.0 * v + (source - 16.0), -1.0)
            Pb[:, block * TOK : (block + 1) * TOK] = jnp.where(io_row == v, 1.0, 0.0).astype(BF)

        def pick(columns):
            both = [
                jnp.dot(
                    Pb[:, cc * 1024 : (cc + 1) * 1024],
                    T[cc, pl.ds(2 * a, 2), :, :, columns].reshape(1024, wide),
                    preferred_element_type=F32,
                )
                for cc in range(2)
            ]
            return both[0] + both[1]

        here = pl.ds(pl.multiple_of(a * 16, 16), 16)

        def tile(n, carry):
            columns = pl.ds(pl.multiple_of(n * wide, wide), wide)
            X[l, :, here, columns] = pick(columns).astype(BF).reshape(CAP, 16, wide)
            return carry

        lax.fori_loop(0, D // wide, tile, 0)
        last = pick(slice(D, EXT))
        lane = lax.broadcasted_iota(jnp.int32, (group, wide), 1)
        gate = jnp.sum(
            jnp.where(lane == EXPERTS + ep * LOCAL + l, last, 0.0), axis=1, keepdims=True
        )
        G[l, :, here, :] = jnp.broadcast_to(gate, (group, 128)).reshape(CAP, 16, 128)
        return carry

    lax.fori_loop(0, 2 * LOCAL, unit, 0)

    def scale(l, carry):
        gate = G[l].reshape(ROWS, 128)
        for n in range(HID // 128):
            columns = slice(n * 128, (n + 1) * 128)
            S[l, :, columns] = (gate * H[l, :, columns].astype(F32)).astype(BF)
        return carry

    lax.fori_loop(0, LOCAL, scale, 0)

    def terms(t, out):
        def expert(l, carry):
            owner = jnp.where(l < 2, (z + 2 * NZ - 1 - t) % NZ, (z + 1 + t) % NZ)
            lhs = X[l, :, :, pl.ds(pl.multiple_of(owner * DS, DS), DS)].reshape(ROWS, DS)
            for n in range(HID // wide):
                columns = slice(n * wide, (n + 1) * wide)
                out[l, :, columns] = lax.dot_general(
                    lhs, S[l, :, columns], (((0,), (0,)), ((), ())), preferred_element_type=F32
                ).astype(BF)
            return carry

        lax.fori_loop(0, LOCAL, expert, 0)

    def rs(t, l, src):
        return pltpu.make_async_remote_copy(
            src_ref=src,
            dst_ref=R.at[t, l],
            send_sem=rs_s.at[t, l],
            recv_sem=rs_r.at[t, l],
            device_id=z_up if l < 2 else z_dn,
            device_id_type=MESH,
        )

    order = (0, 2, 1, 3)
    terms(0, Fst)
    for l in order:
        rs(0, l, Fst.at[l]).start()
    terms(1, Tm)

    def upstream(l, carry):
        slot = jnp.zeros((ROWS, 1), F32)
        gate = jnp.concatenate([G[l].reshape(ROWS, 128)] * (wide // 128), axis=1)
        for n in range(HID // wide):
            columns = slice(n * wide, (n + 1) * wide)
            weights = W[:, :, pl.ds(pl.multiple_of(l * HID + n * wide, wide), wide)]
            u = jnp.dot(
                X[l].reshape(ROWS, D), weights.reshape(D, wide), preferred_element_type=F32
            )
            slot = slot + jnp.sum(H[l, :, columns].astype(F32) * u, axis=1, keepdims=True)
            H[l, :, columns] = (gate * u).astype(BF)
        lane = lax.broadcasted_iota(jnp.int32, (NE, 128), 1)
        mine = SG[c, y, x]
        for s in range(CAP):
            mine = jnp.where(lane == l * 16 + s, slot[s * NE : (s + 1) * NE, :], mine)
        SG[c, y, x] = mine
        return carry

    out_hidden = pltpu.make_async_copy(H, hg_ref, loc.at[3])

    def sg(n, ref, other):
        return pltpu.make_async_remote_copy(
            src_ref=ref,
            dst_ref=ref,
            send_sem=sg_s.at[n],
            recv_sem=sg_r.at[n],
            device_id=other,
            device_id_type=MESH,
        )

    slots = [
        [sg(0, SG.at[c, y, x], to_xu), sg(1, SG.at[c, y, x], to_xd)],
        [sg(2, SG.at[c, y, x_dn], to_xu)],
        [sg(3, SG.at[c, y], to_yu), sg(4, SG.at[c, y], to_yd)],
        [sg(5, SG.at[c, y_dn], to_yu)],
        [sg(6, SG.at[c], sibling)],
    ]

    def pass_on(n):
        if n > 0:
            for copy in slots[n - 1]:
                copy.wait_recv()
        for copy in slots[n]:
            copy.start()

    SG[c, y, x] = jnp.zeros((NE, 128), F32)

    def step(t, carry):
        for l in order:
            rs(t - 1, l, R.at[t - 1, l]).wait_recv()
            R[t - 1, l] = (R[t - 1, l].astype(F32) + Tm[l].astype(F32)).astype(BF)
            rs(t, l, R.at[t - 1, l]).start()
        terms(t + 1, Tm)

        @pl.when(t == 1)
        def _():
            for i in range(4):
                ag(STEPS - 1, i).wait_recv()
            own_w.wait()

        @pl.when(t <= 2)
        def _():
            lax.fori_loop(2 * t - 2, 2 * t, upstream, 0)

        @pl.when(t == 3)
        def _():
            out_hidden.start()
            pass_on(0)

        @pl.when(t == 4)
        def _():
            pass_on(1)

        @pl.when(t == 5)
        def _():
            pass_on(2)

        @pl.when(t == 6)
        def _():
            pass_on(3)

        return carry

    lax.fori_loop(1, STEPS, step, 0)
    pass_on(4)
    slots[4][0].wait_recv()

    row = lax.broadcasted_iota(jnp.int32, (NE, NE, 128), 1)
    by_dev = jnp.sum(jnp.where(row == ep, SG[...].reshape(NE, NE, 128), 0.0), axis=1)
    high = by_dev.astype(BF)
    low = (by_dev - high.astype(F32)).astype(BF)
    io_dev = lax.broadcasted_iota(jnp.int32, (NE, TOK), 0)
    io_in = lax.broadcasted_iota(jnp.int32, (128, TOK), 0)
    for k in range(TOPK):
        q = meta[k : k + 1, :].astype(jnp.int32)
        r = meta[TOPK + k : TOPK + k + 1, :].astype(jnp.int32)
        device = lax.shift_right_logical(q, 2)
        place = lax.bitwise_and(device, 1) * 16 + lax.shift_right_logical(device, 1)
        pickers = (io_dev == place).astype(F32).astype(BF)
        found = sum(
            lax.dot_general(part, pickers, (((0,), (0,)), ((), ())), preferred_element_type=F32)
            for part in (high, low)
        )
        inside = lax.bitwise_and(q, 3) * 16 + r
        gg_ref[k : k + 1, :] = jnp.sum(
            jnp.where(io_in == inside, found, 0.0), axis=0, keepdims=True
        )

    outs = []
    for l in order:
        rs(STEPS - 1, l, R.at[STEPS - 1, l]).wait_recv()
        O[l] = R[STEPS - 1, l].astype(F32) + Tm[l].astype(F32)
        copy = pltpu.make_async_copy(O.at[l], wg_ref.at[:, pl.ds(l * HID, HID)], loc.at[4 + l])
        copy.start()
        outs.append(copy)

    for t in range(STEPS):
        for i in range(4):
            ag(t, i).wait_send()
            rs(t, i, Fst.at[i]).wait_send()
    for copies in tokens + slots:
        for copy in copies:
            copy.wait_send()
    out_hidden.wait()
    for copy in outs:
        copy.wait()


def local(out_grad, gates, routes, expert_slot, hidden_saved, w_down):
    hbm, vmem = pl.BlockSpec(memory_space=pl.ANY), pl.BlockSpec(memory_space=pltpu.VMEM)
    dma = pltpu.SemaphoreType.DMA
    saved = hidden_saved[0].transpose(0, 2, 1, 3).reshape(LOCAL, ROWS, HID)
    hidden_grad, gate_grad, weight_grad = pl.pallas_call(
        kernel,
        out_shape=(
            jax.ShapeDtypeStruct((LOCAL, ROWS, HID), BF),
            jax.ShapeDtypeStruct((TOPK, TOK), F32),
            jax.ShapeDtypeStruct((DS, LOCAL * HID), F32),
        ),
        in_specs=[hbm, hbm, vmem, vmem, vmem, hbm],
        out_specs=(hbm, vmem, hbm),
        scratch_shapes=[
            pltpu.VMEM((NC, NY, NX, TOK, EXT), BF),
            pltpu.VMEM((NZ, DS, LOCAL * HID), BF),
            pltpu.VMEM((LOCAL, CAP, NE, D), BF),
            pltpu.VMEM((LOCAL, CAP, NE, 128), F32),
            pltpu.VMEM((LOCAL, ROWS, HID), BF),
            pltpu.VMEM((LOCAL, ROWS, HID), BF),
            pltpu.VMEM((STEPS, LOCAL, DS, HID), BF),
            pltpu.VMEM((LOCAL, DS, HID), BF),
            pltpu.VMEM((LOCAL, DS, HID), BF),
            pltpu.VMEM((NC, NY, NX, NE, 128), F32),
            pltpu.VMEM((LOCAL, DS, HID), F32),
            pltpu.VMEM((ROWS // 2, 16 * TOK), BF),
            pltpu.VMEM((2 * TOPK, TOK), F32),
            dma((STEPS, 4)),
            dma((STEPS, 4)),
            dma((STEPS, 4)),
            dma((STEPS, 4)),
            dma((18,)),
            dma((18,)),
            dma((7,)),
            dma((7,)),
            dma((8,)),
        ],
        compiler_params=pltpu.CompilerParams(
            collective_id=0, has_side_effects=True, vmem_limit_bytes=66 * 1000 * 1000
        ),
        cost_estimate=pl.CostEstimate(
            flops=20_000_000_000, bytes_accessed=15_000_000, transcendentals=0
        ),
    )(
        w_down,
        out_grad[0],
        routes[0].T,
        gates[0].T,
        expert_slot.reshape(1, EXPERTS),
        saved,
    )
    hidden_grad = hidden_grad.reshape(LOCAL, CAP, NE, HID).transpose(0, 2, 1, 3)[None]
    return hidden_grad, gate_grad.T[None], weight_grad


def solution(mesh):
    return jax.shard_map(
        local,
        mesh=mesh,
        in_specs=(
            P("dp", "ep", None),
            P("dp", "ep", None),
            P("dp", "ep", None),
            P(),
            P("dp", "ep", None, None, None),
            P("dp", "ep"),
        ),
        out_specs=(P("dp", "ep", None, None, None), P("dp", "ep", None), P("dp", "ep")),
        check_vma=False,
    )
```

time: 301 us -> 257 us (0.85)
  Pallas kernels: 0 us -> 247 us
  waiting for transfers between devices: 175 us -> 0 us
  local copies, waits for them, and re-layouts: 53.1 us -> 5.64 us
  matrix products: 25.4 us -> 0 us
  starting transfers between devices: 24.1 us -> 0 us
  between operations: 14.3 us -> 0.66 us
  other arithmetic: 4.91 us -> 0 us
    pallas_call x0 -> x1, Pallas kernels: none -> 247 us  [local(): pl.pallas_call(kernel, out_shape=(jax.ShapeDtypeStruct((LOCAL, ROWS, HID)...]
    reduce_scatter x1 -> x0, waiting for transfers between devices: 95.6 us -> none  [local(): lax.psum_scatter(term.reshape(width // lax.axis_size('dp') * lax.axis_siz...]
    all_to_all x3 -> x0, waiting for transfers between devices: 79.8 us -> none  [the longest x1 72.8 us: local(): lax.all_to_all(send_rows.reshape(n_ep, exp_dev * slots, width), 'ep', spl...]
    dot_general x2 -> x0, matrix products: 25.4 us -> none  [the longest x1 15.5 us: local(): jnp.einsum('slcd,dlj->lscj', recv_rows, w_all, preferred_element_type=jnp...]
    all_to_all x3 -> x0, starting transfers between devices: 24.1 us -> none  [the longest x1 8.69 us: local(): lax.all_to_all(slot_grad.transpose(1, 0, 2).reshape(n_ep, exp_dev * slots...]
    scatter x2 -> x0, local copies, waits for them, and re-layouts: 17.7 us -> none  [the longest x1 10.1 us: local(): jnp.zeros((experts * slots, width), jnp.bfloat16).at[target].set(rows)]
    convert_element_type x3 -> x0, local copies, waits for them, and re-layouts: 16.8 us -> none  [the longest x1 16.7 us: local(): term.reshape(width // lax.axis_size('dp') * lax.axis_size('dp'), exp_dev...]
    all_to_all x5 -> x0, local copies, waits for them, and re-layouts: 8.24 us -> none  [the longest x1 6.35 us: local(): lax.all_to_all(send_rows.reshape(n_ep, exp_dev * slots, width), 'ep', spl...]
  transfers between devices with their start and end apart: 5 -> 0, of which waited for: 3 -> 0; matrix products, arithmetic and copies ran while one was open for 26% -> 0% of each run, Pallas kernels for 0% -> 0%
where the time goes in v1:
time: 257 us; the launch traced here: 254 us
  Pallas kernels  247 us (96%)
  local copies, waits for them, and re-layouts  5.64 us (2%)
    pallas_call x1, Pallas kernels, local(): pl.pallas_call(kernel, out_shape=(jax.ShapeDtypeStruct((LOCAL, ROWS, HID)...  247 us
    unnamed x7, local copies, waits for them, and re-layouts  5.64 us

profile of v1, /device:TPU:33, one launch (start us, length us, event | category | flops | bytes accessed | tf_op | source)
XLA Modules:
  0.0 253.7 jit_solution(15694530727904932574)
XLA Ops:
  0.6 247.4 %shard_map.85 = (bf16[4,384,768]{2,1,0:T(8,128)(2,1)}, f32[8,128]{1,0:T(8,128)}, f32[256,3072]{1,0:T(8,128)}) custom-call(bf16[256,3072]{1,0:T(8,128)(2,1)} %w_ref.1, bf16[128,2048]{1,0:T(8,128)(2,1)} %bitcast.24, s32[8,128]{1,0:T(8,128)} %bitcast.25, bf16[8,128]{1,0:T(8,128)(2,1)} %bitcast.26, s32[1,128]{1,0:T(1,128)} %bitcast.27, bf16[4,384,768]{2,1,0:T(8,128)(2,1)} %bitcast.23), custom_call_target="tpu_custom_call" | custom-call | flops 20000000000 | bytes 15000000 | tf_op jit(solution)/shard_map/pallas_call | solution.py:389
  248.1 0.0 copy-start.1
  248.1 0.0 copy-start
  248.1 3.4 %copy.12 = bf16[1,4,32,12,768]{4,2,3,1,0:T(8,128)(2,1)} copy(bf16[1,4,32,12,768]{4,2,3,1,0:T(8,128)(2,1)} %bitcast.21) | data formatting | bytes 4718592
  251.5 0.0 copy-done.1
  251.5 0.6 copy.13
  252.1 0.0 copy-done
  252.1 1.7 copy.14
Async XLA Ops:
  248.1 3.4 %copy-start.1 = (f32[8,128]{1,0:T(8,128)S(1)}, f32[8,128]{1,0:T(8,128)}, u32[]{:S(2)}) copy-start(f32[8,128]{1,0:T(8,128)} %get-tuple-element.7) | copy-start | bytes 12292
  248.1 4.0 %copy-start = (f32[256,3072]{1,0:T(8,128)S(1)}, f32[256,3072]{1,0:T(8,128)}, u32[]{:S(2)}) copy-start(f32[256,3072]{1,0:T(8,128)} %get-tuple-element.14) | copy-start | bytes 9437188

commit v2 on v1

v2 whole, which is shorter than its diff:
```python
import jax
import jax.numpy as jnp
from jax import lax
from jax.experimental import pallas as pl
from jax.experimental.pallas import tpu as pltpu
from jax.sharding import PartitionSpec as P

BF = jnp.bfloat16
F32 = jnp.float32
MESH = pl.DeviceIdType.MESH
NX, NY, NC, NZ = 4, 4, 2, 8
NE = NX * NY * NC
TOK, D, TOPK = 128, 2048, 8
EXPERTS, LOCAL, CAP, HID = 128, 4, 12, 768
DS = D // NZ
EXT = D + 2 * EXPERTS
ROWS = CAP * NE


def kernel(
    w_ref, og_ref, rt_ref, gt_ref, es_ref, hs_ref,
    hg_ref, gg_ref, wg_ref,
    T, W, X, Xf, G, S, Sf, H, Fst, Tm, Ub, Ur, SG, O, Pb, meta,
    ag_s, ag_r, rs_s, rs_r, tk_s, tk_r, sb_s, sb_r, sg_s, sg_r, ex_s, ex_r, loc, free,
):
    ep, z = lax.axis_index("ep"), lax.axis_index("dp")
    c, x, y = ep % NC, (ep // NC) % NX, ep // (NC * NX)

    def at(yy, xx, cc):
        return ((yy * NX + xx) * NC + cc, z)

    x_up, x_dn = (x + 1) % NX, (x + NX - 1) % NX
    y_up, y_dn = (y + 1) % NY, (y + NY - 1) % NY
    to_xu, to_xd, to_yu, to_yd = at(y, x_up, c), at(y, x_dn, c), at(y_up, x, c), at(y_dn, x, c)
    sibling = at(y, x, 1 - c)

    turn = (z + NZ + 1 - c) % NZ
    odd, pair = turn % 2, turn // 2
    sign = 2 * odd - 1
    role = [(pair + 1 - odd - sign * j + 8) % LOCAL for j in range(LOCAL)]

    def layer(offset):
        return (z + sign * offset + 2 * NZ) % NZ

    side = [(ep, layer(1)), (ep, layer(-1))]
    partner = side[1]
    way = [1 - odd, odd]

    barrier = pltpu.get_barrier_semaphore()
    for other in (side[0], side[1], to_xu, to_xd, to_yu, to_yd, sibling):
        pl.semaphore_signal(barrier, inc=1, device_id=other, device_id_type=MESH)
    pl.semaphore_wait(barrier, 7)

    def ag(flow, t, j):
        owner = layer(-t) if flow == 0 else layer(t)
        l = role[j]
        return pltpu.make_async_remote_copy(
            src_ref=w_ref.at[:, pl.ds(pl.multiple_of(l * HID, HID), HID)] if t == 0 else W.at[l, owner],
            dst_ref=W.at[l, owner],
            send_sem=ag_s.at[flow, j, t],
            recv_sem=ag_r.at[way[flow], l, t],
            device_id=side[flow],
            device_id_type=MESH,
        )

    def ag_list(t):
        fwd = [(0, t, j) for j in (0, 1, 2) if t <= 2 * j + 1]
        bwd = [(1, t, j) for j in (3, 2, 1) if t <= 6 - 2 * j]
        both = []
        for i in range(3):
            both += fwd[i : i + 1] + bwd[i : i + 1]
        return both

    def ag_step(t):
        for flow, t, j in ag_list(t):
            if t > 0:
                ag(flow, t - 1, j).wait_recv()
            ag(flow, t, j).start()

    ag_step(0)
    cx = (c, y, x // 2, x % 2)
    own_tokens = pltpu.make_async_copy(og_ref, T.at[(*cx, slice(None), pl.ds(0, D))], loc.at[0])
    own_tokens.start()
    own_saved = pltpu.make_async_copy(hs_ref, H, loc.at[1])
    own_saved.start()
    own_w = [
        pltpu.make_async_copy(w_ref.at[:, pl.ds(l * HID, HID)], W.at[l, z], loc.at[8 + l])
        for l in range(LOCAL)
    ]
    for copy in own_w:
        copy.start()

    io0 = lax.broadcasted_iota(jnp.int32, (EXPERTS, TOK), 0)
    io1 = lax.broadcasted_iota(jnp.int32, (EXPERTS, TOK), 1)
    es = es_ref[...]
    to_slot = (io0 == es).astype(F32).astype(BF)
    slot_of = jnp.transpose(jnp.broadcast_to(es.astype(F32), (EXPERTS, EXPERTS)))
    named = jnp.zeros((EXPERTS, TOK), F32)
    weight = jnp.zeros((EXPERTS, TOK), F32)
    for k in range(TOPK):
        hit = (io0 == rt_ref[k : k + 1, :]).astype(F32)
        named = named + hit
        weight = weight + hit * gt_ref[k : k + 1, :].astype(F32)
        meta[k : k + 1, :] = jnp.sum(hit * slot_of, axis=0, keepdims=True)
    earlier = (io0 < io1).astype(F32).astype(BF)
    rank = jnp.dot(named.astype(BF), earlier, preferred_element_type=F32)
    for k in range(TOPK):
        hit = (io0 == rt_ref[k : k + 1, :]).astype(F32)
        meta[TOPK + k : TOPK + k + 1, :] = jnp.sum(hit * rank, axis=0, keepdims=True)
    ranks = jnp.dot(to_slot, ((rank + 1.0) * named).astype(BF), preferred_element_type=F32)
    gates = jnp.dot(to_slot, weight.astype(BF), preferred_element_type=F32)
    T[c, y, x // 2, x % 2, :, D : D + EXPERTS] = ranks.astype(BF)
    T[c, y, x // 2, x % 2, :, D + EXPERTS : EXT] = jnp.transpose(gates).astype(BF)
    own_tokens.wait()

    half = TOK // 2
    up_rows, dn_rows = pl.ds(0, half), pl.ds(half, half)
    quarter = [pl.ds(i * half // 2, half // 2) for i in range(4)]
    every = slice(None)
    x_op, y_op = (x + 2) % NX, (y + 2) % NY

    def blocks(yy, xx, rows):
        if xx is every:
            return T.at[c, yy, :, :, rows]
        if yy is every:
            return T.at[c, :, xx // 2, xx % 2, rows]
        return T.at[c, yy, xx // 2, xx % 2, rows]

    def remote(ref, dst, send, recv, other):
        return pltpu.make_async_remote_copy(
            src_ref=ref, dst_ref=dst, send_sem=send, recv_sem=recv, device_id=other, device_id_type=MESH
        )

    def tk(n, ref, other):
        return remote(ref, ref, tk_s.at[n], tk_r.at[n], other)

    def sb(n, ref):
        return remote(ref, ref, sb_s.at[n], sb_r.at[n], sibling)

    tokens = [
        [
            tk(0, blocks(y, x, up_rows), to_xu),
            tk(1, blocks(y, x, up_rows), to_xd),
            tk(2, blocks(y, x, dn_rows), to_yu),
            tk(3, blocks(y, x, dn_rows), to_yd),
        ],
        [
            tk(4, blocks(y, x_dn, quarter[0]), to_xu),
            tk(5, blocks(y, x_up, quarter[1]), to_xd),
            tk(6, blocks(y_dn, x, quarter[2]), to_yu),
            tk(7, blocks(y_up, x, quarter[3]), to_yd),
        ],
        [
            tk(8, blocks(y, every, up_rows), to_yu),
            tk(9, blocks(y, every, up_rows), to_yd),
            tk(10, blocks(every, x, dn_rows), to_xu),
            tk(11, blocks(every, x, dn_rows), to_xd),
        ],
        [
            tk(12, blocks(y_dn, every, quarter[0]), to_yu),
            tk(13, blocks(y_up, every, quarter[1]), to_yd),
            tk(14, blocks(every, x_dn, quarter[2]), to_xu),
            tk(15, blocks(every, x_up, quarter[3]), to_xd),
        ],
        [],
    ]
    across = [
        [sb(0, blocks(y, x, pl.ds(0, TOK)))],
        [
            sb(1, blocks(y, x_dn, up_rows)),
            sb(2, blocks(y, x_up, up_rows)),
            sb(3, blocks(y_dn, x, dn_rows)),
            sb(4, blocks(y_up, x, dn_rows)),
        ],
        [sb(5, blocks(y, x_op, up_rows)), sb(6, blocks(y_op, x, dn_rows))],
        [
            sb(7, blocks(y_dn, every, up_rows)),
            sb(8, blocks(y_up, every, up_rows)),
            sb(9, blocks(every, x_dn, dn_rows)),
            sb(10, blocks(every, x_up, dn_rows)),
        ],
        [sb(11, blocks(y_op, every, up_rows)), sb(12, blocks(every, x_op, dn_rows))],
    ]

    def phase(n):
        if n > 0:
            for copy in tokens[n - 1]:
                copy.wait_recv()
        for copy in tokens[n] + across[n]:
            copy.start()

    phase(0)
    phase(1)
    phase(2)
    ag_step(1)
    phase(3)
    ag_step(2)
    phase(4)
    own_saved.wait()
    for copies in across:
        for copy in copies:
            copy.wait_recv()

    group = ROWS // 2
    io_row = lax.broadcasted_iota(jnp.int32, (group, TOK), 0).astype(F32)
    io16 = lax.broadcasted_iota(jnp.int32, (16, TOK), 0)
    first = pl.multiple_of((ep // 4) * 16, 16)
    wide = 256

    def pick_rows(l, a):
        for block in range(16):
            cc, yy, xx = block // 8, (block // 4) % 2, block % 4
            sixteen = T[cc, 2 * a + yy, xx // 2, xx % 2, pl.ds(first, 16), D : D + EXPERTS].astype(F32)
            v = jnp.sum(
                jnp.where(io16 == (ep % 4) * 4 + l, sixteen, 0.0), axis=0, keepdims=True
            )
            source = (yy * NX + xx) * NC + cc
            v = jnp.where(v > 0.5, 16.0 * v + (source - 16.0), -1.0)
            Pb[:, block * TOK : (block + 1) * TOK] = jnp.where(io_row == v, 1.0, 0.0).astype(BF)

        def pick(columns):
            both = [
                jnp.dot(
                    Pb[:, cc * 1024 : (cc + 1) * 1024],
                    T[cc, pl.ds(2 * a, 2), :, :, :, columns].reshape(1024, wide),
                    preferred_element_type=F32,
                )
                for cc in range(2)
            ]
            return both[0] + both[1]

        here = pl.ds(pl.multiple_of(a * 16, 16), 16)

        def tile(n, carry):
            columns = pl.ds(pl.multiple_of(n * wide, wide), wide)
            X[l, :, here, columns] = pick(columns).astype(BF).reshape(CAP, 16, wide)
            return carry

        lax.fori_loop(0, D // wide, tile, 0)
        last = pick(slice(D, EXT))
        lane = lax.broadcasted_iota(jnp.int32, (group, wide), 1)
        gate = jnp.sum(
            jnp.where(lane == EXPERTS + ep * LOCAL + l, last, 0.0), axis=1, keepdims=True
        )
        G[l, :, here, :] = jnp.broadcast_to(gate, (group, 128)).reshape(CAP, 16, 128)

    def build(j, carry):
        l = (pair + 1 - odd - sign * j + 8) % LOCAL

        def part(a, carry):
            pick_rows(l, a)
            return carry

        lax.fori_loop(0, 2, part, 0)
        gate = G[l].reshape(ROWS, 128)
        for n in range(HID // 128):
            columns = slice(n * 128, (n + 1) * 128)
            S[l, :, columns] = (gate * H[l, :, columns].astype(F32)).astype(BF)
        return carry

    give_rows = remote(X.at[role[3]], Xf, ex_s.at[0], ex_r.at[0], partner)
    give_scaled = remote(S.at[role[3]], Sf, ex_s.at[1], ex_r.at[1], partner)

    def build_and_serve(n, carry):
        build(3 - n, carry)

        @pl.when(n == 0)
        def _():
            give_scaled.start()
            give_rows.start()
            ag_step(3)

        @pl.when(n == 1)
        def _():
            ag_step(4)

        @pl.when(n == 2)
        def _():
            ag_step(5)

        return carry

    lax.fori_loop(0, LOCAL, build_and_serve, 0)

    for copies in tokens + across:
        for copy in copies:
            copy.wait_send()
    for other in side:
        pl.semaphore_signal(free, inc=1, device_id=other, device_id_type=MESH)

    def landing(l, slot):
        n = l * 9 + slot
        j = n // 3
        columns = pl.ds(pl.multiple_of((n % 3) * HID, HID), HID)
        return (j // 8, (j // 2) % 4, j % 2, slice(None), slice(None), columns)

    def term(j, offset, out, index):
        l, owner = role[j], layer(offset)
        there = pl.ds(pl.multiple_of(owner * DS, DS), DS)
        lhs = X[l, :, :, there].reshape(ROWS, DS)
        other = Xf[:, :, there].reshape(ROWS, DS) if j == 0 else None

        def tile(n, carry):
            columns = pl.ds(pl.multiple_of(n * wide, wide), wide)
            dims = (((0,), (0,)), ((), ()))
            both = lax.dot_general(lhs, S[l, :, columns], dims, preferred_element_type=F32)
            if j == 0:
                both = both + lax.dot_general(
                    other, Sf[:, columns], dims, preferred_element_type=F32
                )
            out[index, :, :, columns] = both.astype(BF).reshape(2, DS // 2, wide)
            return carry

        lax.fori_loop(0, HID // wide, tile, 0)

    def rs(flow, t, j, src):
        slot = 8 - t + 2 * j if flow == 0 else t - 5 + 2 * j
        return remote(
            src,
            T.at[landing(role[j], slot)],
            rs_s.at[flow, j, t],
            rs_r.at[way[flow], role[j], t],
            side[flow],
        )

    def arrived(flow, t, j):
        slot = t - (2 * j - 1) if flow == 0 else 12 - t - 2 * j
        ref = T.at[landing(role[j], slot)]
        remote(ref, ref, rs_s.at[flow, j, t], rs_r.at[way[flow], role[j], t], side[flow]).wait_recv()
        return landing(role[j], slot)

    def reach(flow, t):
        return 6 - t if flow == 0 else t - 6

    def rs_list(t):
        fwd = [(0, j) for j in (2, 1) if t >= 2 * j]
        bwd = [(1, j) for j in (0, 1, 2) if t >= 5 - 2 * j]
        return bwd + fwd if t < 2 else [v for p in zip(fwd + [None] * 3, bwd + [None] * 3) for v in p if v]

    sends = []

    def start(t):
        term(0, 6 - t, Fst, t)
        copy = rs(0, t, 0, Fst.at[t])
        copy.start()
        sends.append(copy)

    def rs_step(t):
        for flow, j in rs_list(t):
            here = arrived(flow, t - 1, j)
            T[here] = (T[here].astype(F32) + Tm[flow * 3 + j].astype(F32)).astype(BF)
            copy = rs(flow, t, j, T.at[here])
            copy.start()
            sends.append(copy)
        for flow, j in rs_list(t):
            if t < 5:
                term(j, reach(flow, t + 1), Tm, flow * 3 + j)

    term(2, reach(1, 1), Tm, 5)
    term(1, reach(0, 2), Tm, 1)
    term(1, reach(1, 3), Tm, 4)
    term(2, reach(0, 4), Tm, 2)
    pl.semaphore_wait(free, 2)
    give_scaled.wait_recv()
    give_rows.wait_recv()
    start(0)
    start(1)
    start(2)

    def u_tile(rows, l, n):
        columns = pl.ds(pl.multiple_of(n * wide, wide), wide)
        weights = W[l, :, :, columns].reshape(D, wide)
        return columns, jnp.dot(rows, weights, preferred_element_type=F32)

    def note(l, slot):
        lane = lax.broadcasted_iota(jnp.int32, (NE, 128), 1)
        mine = SG[c, y, x]
        for s in range(CAP):
            mine = jnp.where(lane == l * 16 + s, slot[s * NE : (s + 1) * NE, :], mine)
        SG[c, y, x] = mine

    def upstream(j, carry):
        l = (pair + 1 - odd - sign * j + 8) % LOCAL
        gate = jnp.concatenate([G[l].reshape(ROWS, 128)] * (wide // 128), axis=1)

        def tile(n, slot):
            columns, u = u_tile(X[l].reshape(ROWS, D), l, n)
            slot = slot + jnp.sum(H[l, :, columns].astype(F32) * u, axis=1, keepdims=True)
            H[l, :, columns] = (gate * u).astype(BF)
            return slot

        note(l, lax.fori_loop(0, HID // wide, tile, jnp.zeros((ROWS, 1), F32)))
        return carry

    def upstream_given():
        def tile(n, carry):
            columns, u = u_tile(Xf[...].reshape(ROWS, D), role[0], n)
            Ub[:, columns] = u.astype(BF)
            return carry

        lax.fori_loop(0, HID // wide, tile, 0)

    def upstream_away():
        l = role[3]
        gate = G[l].reshape(ROWS, 128)
        slot = jnp.zeros((ROWS, 1), F32)
        for n in range(HID // 128):
            columns = slice(n * 128, (n + 1) * 128)
            u = Ur[:, columns].astype(F32)
            slot = slot + jnp.sum(H[l, :, columns].astype(F32) * u, axis=1, keepdims=True)
            H[l, :, columns] = (gate * u).astype(BF)
        note(l, slot)

    out_hidden = pltpu.make_async_copy(H, hg_ref, loc.at[3])
    give_u = remote(Ub, Ur, ex_s.at[2], ex_r.at[2], partner)

    def sg(n, ref, other):
        return remote(ref, ref, sg_s.at[n], sg_r.at[n], other)

    slots = [
        [sg(0, SG.at[c, y, x], to_xu), sg(1, SG.at[c, y, x], to_xd)],
        [sg(2, SG.at[c, y, x_dn], to_xu)],
        [sg(3, SG.at[c, y], to_yu), sg(4, SG.at[c, y], to_yd)],
        [sg(5, SG.at[c, y_dn], to_yu)],
        [sg(6, SG.at[c], sibling)],
    ]

    def pass_on(n):
        if n > 0:
            for copy in slots[n - 1]:
                copy.wait_recv()
        for copy in slots[n]:
            copy.start()

    SG[c, y, x] = jnp.zeros((NE, 128), F32)

    rs_step(1)
    start(3)
    for t in range(6):
        ag(1, t, 0).wait_recv()
    for copy in own_w:
        copy.wait()
    upstream_given()
    give_u.start()
    rs_step(2)
    start(4)
    upstream(2, 0)
    rs_step(3)
    start(5)
    lax.fori_loop(0, 2, upstream, 0)
    rs_step(4)
    term(0, reach(1, 5), Tm, 3)
    give_u.wait_recv()
    upstream_away()
    out_hidden.start()
    pass_on(0)
    rs_step(5)
    pass_on(1)
    for j in range(3):
        term(j, 0, Tm, j)
    pass_on(2)
    pass_on(3)
    pass_on(4)
    slots[4][0].wait_recv()

    row = lax.broadcasted_iota(jnp.int32, (NE, NE, 128), 1)
    by_dev = jnp.sum(jnp.where(row == ep, SG[...].reshape(NE, NE, 128), 0.0), axis=1)
    high = by_dev.astype(BF)
    low = (by_dev - high.astype(F32)).astype(BF)
    io_dev = lax.broadcasted_iota(jnp.int32, (NE, TOK), 0)
    io_in = lax.broadcasted_iota(jnp.int32, (128, TOK), 0)
    for k in range(TOPK):
        q = meta[k : k + 1, :].astype(jnp.int32)
        r = meta[TOPK + k : TOPK + k + 1, :].astype(jnp.int32)
        device = lax.shift_right_logical(q, 2)
        place = lax.bitwise_and(device, 1) * 16 + lax.shift_right_logical(device, 1)
        pickers = (io_dev == place).astype(F32).astype(BF)
        found = sum(
            lax.dot_general(part, pickers, (((0,), (0,)), ((), ())), preferred_element_type=F32)
            for part in (high, low)
        )
        inside = lax.bitwise_and(q, 3) * 16 + r
        gg_ref[k : k + 1, :] = jnp.sum(
            jnp.where(io_in == inside, found, 0.0), axis=0, keepdims=True
        )

    outs = []
    for j, flows in ((3, (0,)), (2, (0, 1)), (1, (0, 1)), (0, (1,))):
        total = Tm[j].astype(F32) if j < 3 else None
        for flow in flows:
            part = T[arrived(flow, 5, j)].astype(F32)
            total = part if total is None else total + part
        l = role[j]
        O[l] = total.reshape(DS, HID)
        copy = pltpu.make_async_copy(
            O.at[l], wg_ref.at[:, pl.ds(pl.multiple_of(l * HID, HID), HID)], loc.at[4 + j]
        )
        copy.start()
        outs.append(copy)

    for t in range(6):
        for flow, t, j in ag_list(t):
            ag(flow, t, j).wait_send()
    for copy in sends + [give_scaled, give_rows, give_u]:
        copy.wait_send()
    for copies in slots:
        for copy in copies:
            copy.wait_send()
    out_hidden.wait()
    for copy in outs:
        copy.wait()


def local(out_grad, gates, routes, expert_slot, hidden_saved, w_down):
    hbm, vmem = pl.BlockSpec(memory_space=pl.ANY), pl.BlockSpec(memory_space=pltpu.VMEM)
    dma = pltpu.SemaphoreType.DMA
    saved = hidden_saved[0].transpose(0, 2, 1, 3).reshape(LOCAL, ROWS, HID)
    hidden_grad, gate_grad, weight_grad = pl.pallas_call(
        kernel,
        out_shape=(
            jax.ShapeDtypeStruct((LOCAL, ROWS, HID), BF),
            jax.ShapeDtypeStruct((TOPK, TOK), F32),
            jax.ShapeDtypeStruct((DS, LOCAL * HID), F32),
        ),
        in_specs=[hbm, hbm, vmem, vmem, vmem, hbm],
        out_specs=(hbm, vmem, hbm),
        scratch_shapes=[
            pltpu.VMEM((NC, NY, NX // 2, 2, TOK, EXT), BF),
            pltpu.VMEM((LOCAL, NZ, DS, HID), BF),
            pltpu.VMEM((LOCAL, CAP, NE, D), BF),
            pltpu.VMEM((CAP, NE, D), BF),
            pltpu.VMEM((LOCAL, CAP, NE, 128), F32),
            pltpu.VMEM((LOCAL, ROWS, HID), BF),
            pltpu.VMEM((ROWS, HID), BF),
            pltpu.VMEM((LOCAL, ROWS, HID), BF),
            pltpu.VMEM((6, 2, DS // 2, HID), BF),
            pltpu.VMEM((6, 2, DS // 2, HID), BF),
            pltpu.VMEM((ROWS, HID), BF),
            pltpu.VMEM((ROWS, HID), BF),
            pltpu.VMEM((NC, NY, NX, NE, 128), F32),
            pltpu.VMEM((LOCAL, DS, HID), F32),
            pltpu.VMEM((ROWS // 2, 16 * TOK), BF),
            pltpu.VMEM((2 * TOPK, TOK), F32),
            dma((2, LOCAL, 6)),
            dma((2, LOCAL, 6)),
            dma((2, LOCAL, 6)),
            dma((2, LOCAL, 6)),
            dma((16,)),
            dma((16,)),
            dma((13,)),
            dma((13,)),
            dma((7,)),
            dma((7,)),
            dma((3,)),
            dma((3,)),
            dma((12,)),
            pltpu.SemaphoreType.REGULAR,
        ],
        compiler_params=pltpu.CompilerParams(
            collective_id=0, has_side_effects=True, vmem_limit_bytes=66 * 1000 * 1000
        ),
        cost_estimate=pl.CostEstimate(
            flops=20_000_000_000, bytes_accessed=15_000_000, transcendentals=0
        ),
    )(
        w_down,
        out_grad[0],
        routes[0].T,
        gates[0].T,
        expert_slot.reshape(1, EXPERTS),
        saved,
    )
    hidden_grad = hidden_grad.reshape(LOCAL, CAP, NE, HID).transpose(0, 2, 1, 3)[None]
    return hidden_grad, gate_grad.T[None], weight_grad


def solution(mesh):
    return jax.shard_map(
        local,
        mesh=mesh,
        in_specs=(
            P("dp", "ep", None),
            P("dp", "ep", None),
            P("dp", "ep", None),
            P(),
            P("dp", "ep", None, None, None),
            P("dp", "ep"),
        ),
        out_specs=(P("dp", "ep", None, None, None), P("dp", "ep", None), P("dp", "ep")),
        check_vma=False,
    )
```

time: 257 us -> 240 us (0.934); the launches traced: 254 us -> 240 us
  Pallas kernels: 247 us -> 233 us
    pallas_call x1, Pallas kernels: 247 us -> 233 us  [local(): pl.pallas_call(kernel, out_shape=(jax.ShapeDtypeStruct((LOCAL, ROWS, HID)...]
where the time goes in v2:
time: 240 us
  Pallas kernels  233 us (97%)
  local copies, waits for them, and re-layouts  5.64 us (2%)
    pallas_call x1, Pallas kernels, local(): pl.pallas_call(kernel, out_shape=(jax.ShapeDtypeStruct((LOCAL, ROWS, HID)...  233 us
    unnamed x7, local copies, waits for them, and re-layouts  5.64 us

profile of v2, /device:TPU:33, one launch (start us, length us, event | category | flops | bytes accessed | tf_op | source)
XLA Modules:
  0.0 239.8 jit_solution(2342609976815997338)
XLA Ops:
  0.6 233.5 %shard_map.85 = (bf16[4,384,768]{2,1,0:T(8,128)(2,1)}, f32[8,128]{1,0:T(8,128)}, f32[256,3072]{1,0:T(8,128)}) custom-call(bf16[256,3072]{1,0:T(8,128)(2,1)} %w_ref.1, bf16[128,2048]{1,0:T(8,128)(2,1)} %bitcast.24, s32[8,128]{1,0:T(8,128)} %bitcast.25, bf16[8,128]{1,0:T(8,128)(2,1)} %bitcast.26, s32[1,128]{1,0:T(1,128)} %bitcast.27, bf16[4,384,768]{2,1,0:T(8,128)(2,1)} %bitcast.23), custom_call_target="tpu_custom_call" | custom-call | flops 20000000000 | bytes 15000000 | tf_op jit(solution)/shard_map/pallas_call | solution.py:518
  234.1 0.0 copy-start.1
  234.1 0.0 copy-start
  234.1 3.4 %copy.12 = bf16[1,4,32,12,768]{4,2,3,1,0:T(8,128)(2,1)} copy(bf16[1,4,32,12,768]{4,2,3,1,0:T(8,128)(2,1)} %bitcast.21) | data formatting | bytes 4718592
  237.5 0.0 copy-done.1
  237.5 0.6 copy.13
  238.1 0.0 copy-done
  238.1 1.7 copy.14
Async XLA Ops:
  234.1 3.4 %copy-start.1 = (f32[8,128]{1,0:T(8,128)S(1)}, f32[8,128]{1,0:T(8,128)}, u32[]{:S(2)}) copy-start(f32[8,128]{1,0:T(8,128)} %get-tuple-element.7) | copy-start | bytes 12292
  234.1 4.0 %copy-start = (f32[256,3072]{1,0:T(8,128)S(1)}, f32[256,3072]{1,0:T(8,128)}, u32[]{:S(2)}) copy-start(f32[256,3072]{1,0:T(8,128)} %get-tuple-element.14) | copy-start | bytes 9437188

commit v3 on v2

--- a/solution.py
+++ b/solution.py
@@ -19,8 +19,8 @@
 
 def kernel(
     w_ref, og_ref, rt_ref, gt_ref, es_ref, hs_ref,
-    hg_ref, gg_ref, wg_ref,
-    T, W, X, Xf, G, S, Sf, H, Fst, Tm, Ub, Ur, SG, O, Pb, meta,
+    H, gg_ref, O,
+    T, W, X, Xf, G, S, Sf, Fst, Tm, Ub, Ur, SG, Pb, meta,
     ag_s, ag_r, rs_s, rs_r, tk_s, tk_r, sb_s, sb_r, sg_s, sg_r, ex_s, ex_r, loc, free,
 ):
     ep, z = lax.axis_index("ep"), lax.axis_index("dp")
@@ -207,21 +207,25 @@
     first = pl.multiple_of((ep // 4) * 16, 16)
     wide = 256
 
-    def pick_rows(l, a):
+    def pick_rows(ls, a):
+        tall = len(ls) * group
         for block in range(16):
             cc, yy, xx = block // 8, (block // 4) % 2, block % 4
             sixteen = T[cc, 2 * a + yy, xx // 2, xx % 2, pl.ds(first, 16), D : D + EXPERTS].astype(F32)
-            v = jnp.sum(
-                jnp.where(io16 == (ep % 4) * 4 + l, sixteen, 0.0), axis=0, keepdims=True
-            )
             source = (yy * NX + xx) * NC + cc
-            v = jnp.where(v > 0.5, 16.0 * v + (source - 16.0), -1.0)
-            Pb[:, block * TOK : (block + 1) * TOK] = jnp.where(io_row == v, 1.0, 0.0).astype(BF)
+            for i, l in enumerate(ls):
+                v = jnp.sum(
+                    jnp.where(io16 == (ep % 4) * 4 + l, sixteen, 0.0), axis=0, keepdims=True
+                )
+                v = jnp.where(v > 0.5, 16.0 * v + (source - 16.0), -1.0)
+                Pb[i * group : (i + 1) * group, block * TOK : (block + 1) * TOK] = jnp.where(
+                    io_row == v, 1.0, 0.0
+                ).astype(BF)
 
         def pick(columns):
             both = [
                 jnp.dot(
-                    Pb[:, cc * 1024 : (cc + 1) * 1024],
+                    Pb[:tall, cc * 1024 : (cc + 1) * 1024],
                     T[cc, pl.ds(2 * a, 2), :, :, :, columns].reshape(1024, wide),
                     preferred_element_type=F32,
                 )
@@ -229,58 +233,49 @@
             ]
             return both[0] + both[1]
 
-        here = pl.ds(pl.multiple_of(a * 16, 16), 16)
+        here = pl.ds(a * 16, 16)
 
         def tile(n, carry):
             columns = pl.ds(pl.multiple_of(n * wide, wide), wide)
-            X[l, :, here, columns] = pick(columns).astype(BF).reshape(CAP, 16, wide)
+            rows = pick(columns).astype(BF)
+            for i, l in enumerate(ls):
+                X[l, :, here, columns] = rows[i * group : (i + 1) * group].reshape(CAP, 16, wide)
             return carry
 
         lax.fori_loop(0, D // wide, tile, 0)
         last = pick(slice(D, EXT))
         lane = lax.broadcasted_iota(jnp.int32, (group, wide), 1)
-        gate = jnp.sum(
-            jnp.where(lane == EXPERTS + ep * LOCAL + l, last, 0.0), axis=1, keepdims=True
-        )
-        G[l, :, here, :] = jnp.broadcast_to(gate, (group, 128)).reshape(CAP, 16, 128)
-
-    def build(j, carry):
-        l = (pair + 1 - odd - sign * j + 8) % LOCAL
-
-        def part(a, carry):
-            pick_rows(l, a)
-            return carry
-
-        lax.fori_loop(0, 2, part, 0)
+        for i, l in enumerate(ls):
+            gate = jnp.sum(
+                jnp.where(
+                    lane == EXPERTS + ep * LOCAL + l, last[i * group : (i + 1) * group], 0.0
+                ),
+                axis=1,
+                keepdims=True,
+            )
+            G[l, :, here, :] = jnp.broadcast_to(gate, (group, 128)).reshape(CAP, 16, 128)
+
+    def scale(l):
         gate = G[l].reshape(ROWS, 128)
         for n in range(HID // 128):
             columns = slice(n * 128, (n + 1) * 128)
             S[l, :, columns] = (gate * H[l, :, columns].astype(F32)).astype(BF)
-        return carry
 
     give_rows = remote(X.at[role[3]], Xf, ex_s.at[0], ex_r.at[0], partner)
     give_scaled = remote(S.at[role[3]], Sf, ex_s.at[1], ex_r.at[1], partner)
 
-    def build_and_serve(n, carry):
-        build(3 - n, carry)
-
-        @pl.when(n == 0)
-        def _():
-            give_scaled.start()
-            give_rows.start()
-            ag_step(3)
-
-        @pl.when(n == 1)
-        def _():
-            ag_step(4)
-
-        @pl.when(n == 2)
-        def _():
-            ag_step(5)
-
-        return carry
-
-    lax.fori_loop(0, LOCAL, build_and_serve, 0)
+    pick_rows(role[3:], 0)
+    pick_rows(role[3:], 1)
+    give_rows.start()
+    scale(role[3])
+    give_scaled.start()
+    ag_step(3)
+    pick_rows(role[:3], 0)
+    ag_step(4)
+    pick_rows(role[:3], 1)
+    ag_step(5)
+    for l in role[:3]:
+        scale(l)
 
     for copies in tokens + across:
         for copy in copies:
@@ -411,7 +406,6 @@
             H[l, :, columns] = (gate * u).astype(BF)
         note(l, slot)
 
-    out_hidden = pltpu.make_async_copy(H, hg_ref, loc.at[3])
     give_u = remote(Ub, Ur, ex_s.at[2], ex_r.at[2], partner)
 
     def sg(n, ref, other):
@@ -452,7 +446,6 @@
     term(0, reach(1, 5), Tm, 3)
     give_u.wait_recv()
     upstream_away()
-    out_hidden.start()
     pass_on(0)
     rs_step(5)
     pass_on(1)
@@ -484,19 +477,13 @@
             jnp.where(io_in == inside, found, 0.0), axis=0, keepdims=True
         )
 
-    outs = []
     for j, flows in ((3, (0,)), (2, (0, 1)), (1, (0, 1)), (0, (1,))):
         total = Tm[j].astype(F32) if j < 3 else None
         for flow in flows:
             part = T[arrived(flow, 5, j)].astype(F32)
             total = part if total is None else total + part
         l = role[j]
-        O[l] = total.reshape(DS, HID)
-        copy = pltpu.make_async_copy(
-            O.at[l], wg_ref.at[:, pl.ds(pl.multiple_of(l * HID, HID), HID)], loc.at[4 + j]
-        )
-        copy.start()
-        outs.append(copy)
+        O[:, pl.ds(pl.multiple_of(l * HID, HID), HID)] = total.reshape(DS, HID)
 
     for t in range(6):
         for flow, t, j in ag_list(t):
@@ -506,9 +493,6 @@
     for copies in slots:
         for copy in copies:
             copy.wait_send()
-    out_hidden.wait()
-    for copy in outs:
-        copy.wait()
 
 
 def local(out_grad, gates, routes, expert_slot, hidden_saved, w_down):
@@ -518,12 +502,12 @@
     hidden_grad, gate_grad, weight_grad = pl.pallas_call(
         kernel,
         out_shape=(
-            jax.ShapeDtypeStruct((LOCAL, ROWS, HID), BF),
-            jax.ShapeDtypeStruct((TOPK, TOK), F32),
-            jax.ShapeDtypeStruct((DS, LOCAL * HID), F32),
+            pltpu.VMEM((LOCAL, ROWS, HID), BF),
+            pltpu.VMEM((TOPK, TOK), F32),
+            pltpu.VMEM((DS, LOCAL * HID), F32),
         ),
         in_specs=[hbm, hbm, vmem, vmem, vmem, hbm],
-        out_specs=(hbm, vmem, hbm),
+        out_specs=(vmem, vmem, vmem),
         scratch_shapes=[
             pltpu.VMEM((NC, NY, NX // 2, 2, TOK, EXT), BF),
             pltpu.VMEM((LOCAL, NZ, DS, HID), BF),
@@ -532,14 +516,12 @@
             pltpu.VMEM((LOCAL, CAP, NE, 128), F32),
             pltpu.VMEM((LOCAL, ROWS, HID), BF),
             pltpu.VMEM((ROWS, HID), BF),
-            pltpu.VMEM((LOCAL, ROWS, HID), BF),
             pltpu.VMEM((6, 2, DS // 2, HID), BF),
             pltpu.VMEM((6, 2, DS // 2, HID), BF),
             pltpu.VMEM((ROWS, HID), BF),
             pltpu.VMEM((ROWS, HID), BF),
             pltpu.VMEM((NC, NY, NX, NE, 128), F32),
-            pltpu.VMEM((LOCAL, DS, HID), F32),
-            pltpu.VMEM((ROWS // 2, 16 * TOK), BF),
+            pltpu.VMEM((3 * ROWS // 2, 16 * TOK), BF),
             pltpu.VMEM((2 * TOPK, TOK), F32),
             dma((2, LOCAL, 6)),
             dma((2, LOCAL, 6)),
@@ -557,7 +539,7 @@
             pltpu.SemaphoreType.REGULAR,
         ],
         compiler_params=pltpu.CompilerParams(
-            collective_id=0, has_side_effects=True, vmem_limit_bytes=66 * 1000 * 1000
+            collective_id=0, has_side_effects=True, vmem_limit_bytes=57 * 1000 * 1000
         ),
         cost_estimate=pl.CostEstimate(
             flops=20_000_000_000, bytes_accessed=15_000_000, transcendentals=0

time: 240 us -> 229 us (0.954)
  Pallas kernels: 233 us -> 225 us
    pallas_call x1, Pallas kernels: 233 us -> 225 us  [local(): pl.pallas_call(kernel, out_shape=(pltpu.VMEM((LOCAL, ROWS, HID), BF), plt...]
    unnamed x7 -> x3, local copies, waits for them, and re-layouts: 5.64 us -> 3.66 us
where the time goes in v3:
time: 229 us
  Pallas kernels  225 us (98%)
  local copies, waits for them, and re-layouts  3.66 us (2%)
    pallas_call x1, Pallas kernels, local(): pl.pallas_call(kernel, out_shape=(pltpu.VMEM((LOCAL, ROWS, HID), BF), plt...  225 us

profile of v3, /device:TPU:33, one launch (start us, length us, event | category | flops | bytes accessed | tf_op | source)
XLA Modules:
  0.0 229.1 jit_solution(12593567817521168779)
XLA Ops:
  0.6 224.8 %shard_map.85 = (bf16[4,384,768]{2,1,0:T(8,128)(2,1)S(1)}, f32[8,128]{1,0:T(8,128)S(1)}, f32[256,3072]{1,0:T(8,128)S(1)}) custom-call(bf16[256,3072]{1,0:T(8,128)(2,1)} %w_ref.1, bf16[128,2048]{1,0:T(8,128)(2,1)} %bitcast.24, s32[8,128]{1,0:T(8,128)} %bitcast.25, bf16[8,128]{1,0:T(8,128)(2,1)} %bitcast.26, s32[1,128]{1,0:T(1,128)} %bitcast.27, ...), custom_call_target="tpu_custom_call" | custom-call | flops 20000000000 | bytes 15000000 | tf_op jit(solution)/shard_map/pallas_call | solution.py:502
  225.4 1.4 copy.12
  226.8 0.6 copy.13
  227.4 1.7 copy.14

commit v4 on v3

--- a/solution.py
+++ b/solution.py
@@ -271,9 +271,7 @@
     give_scaled.start()
     ag_step(3)
     pick_rows(role[:3], 0)
-    ag_step(4)
     pick_rows(role[:3], 1)
-    ag_step(5)
     for l in role[:3]:
         scale(l)
 
@@ -360,6 +358,7 @@
     give_rows.wait_recv()
     start(0)
     start(1)
+    ag_step(4)
     start(2)
 
     def u_tile(rows, l, n):
@@ -430,19 +429,20 @@
 
     rs_step(1)
     start(3)
+    ag_step(5)
+    rs_step(2)
+    start(4)
     for t in range(6):
         ag(1, t, 0).wait_recv()
     for copy in own_w:
         copy.wait()
     upstream_given()
     give_u.start()
-    rs_step(2)
-    start(4)
-    upstream(2, 0)
     rs_step(3)
     start(5)
+    upstream(2, 0)
+    rs_step(4)
     lax.fori_loop(0, 2, upstream, 0)
-    rs_step(4)
     term(0, reach(1, 5), Tm, 3)
     give_u.wait_recv()
     upstream_away()
@@ -493,6 +493,15 @@
     for copies in slots:
         for copy in copies:
             copy.wait_send()
+
+
+def write(h_ref, g_ref, w_ref, h_out, g_out, w_out, sem):
+    pairs = ((w_ref, w_out), (h_ref, h_out), (g_ref, g_out))
+    copies = [pltpu.make_async_copy(a, b, sem.at[i]) for i, (a, b) in enumerate(pairs)]
+    for copy in copies:
+        copy.start()
+    for copy in copies:
+        copy.wait()
 
 
 def local(out_grad, gates, routes, expert_slot, hidden_saved, w_down):
@@ -552,6 +561,18 @@
         expert_slot.reshape(1, EXPERTS),
         saved,
     )
+    hidden_grad, gate_grad, weight_grad = pl.pallas_call(
+        write,
+        out_shape=(
+            jax.ShapeDtypeStruct((LOCAL, ROWS, HID), BF),
+            jax.ShapeDtypeStruct((TOPK, TOK), F32),
+            jax.ShapeDtypeStruct((DS, LOCAL * HID), F32),
+        ),
+        in_specs=[vmem, vmem, vmem],
+        out_specs=(hbm, hbm, hbm),
+        scratch_shapes=[dma((3,))],
+        compiler_params=pltpu.CompilerParams(vmem_limit_bytes=1000 * 1000),
+    )(hidden_grad, gate_grad, weight_grad)
     hidden_grad = hidden_grad.reshape(LOCAL, CAP, NE, HID).transpose(0, 2, 1, 3)[None]
     return hidden_grad, gate_grad.T[None], weight_grad
 

time: 229 us -> 223 us (0.974)
  Pallas kernels: 225 us -> 221 us
  local copies, waits for them, and re-layouts: 3.66 us -> 0 us
    pallas_call x1, Pallas kernels: 225 us -> 219 us  [local(): pl.pallas_call(kernel, out_shape=(pltpu.VMEM((LOCAL, ROWS, HID), BF), plt...]
    unnamed x3 -> x0, local copies, waits for them, and re-layouts: 3.66 us -> none
    pallas_call x0 -> x1, Pallas kernels: none -> 2.47 us  [local(): pl.pallas_call(write, out_shape=(jax.ShapeDtypeStruct((LOCAL, ROWS, HID),...]
where the time goes in v4:
time: 223 us; the launch traced here: 222 us
  Pallas kernels  221 us (99%)
    pallas_call x1, Pallas kernels, local(): pl.pallas_call(kernel, out_shape=(pltpu.VMEM((LOCAL, ROWS, HID), BF), plt...  219 us

profile of v4, /device:TPU:33, one launch (start us, length us, event | category | flops | bytes accessed | tf_op | source)
XLA Modules:
  0.0 221.8 jit_solution(14083425174801311792)
XLA Ops:
  0.6 218.6 %shard_map.85 = (bf16[4,384,768]{2,1,0:T(8,128)(2,1)S(1)}, f32[8,128]{1,0:T(8,128)S(1)}, f32[256,3072]{1,0:T(8,128)S(1)}) custom-call(bf16[256,3072]{1,0:T(8,128)(2,1)} %w_ref.1, bf16[128,2048]{1,0:T(8,128)(2,1)} %bitcast.23, s32[8,128]{1,0:T(8,128)} %bitcast.24, bf16[8,128]{1,0:T(8,128)(2,1)} %bitcast.26, s32[1,128]{1,0:T(1,128)} %bitcast.27, ...), custom_call_target="tpu_custom_call" | custom-call | flops 20000000000 | bytes 15000000 | tf_op jit(solution)/shard_map/pallas_call | solution.py:511
  219.2 2.5 %shard_map.86 = (bf16[4,384,768]{2,1,0:T(8,128)(2,1)}, f32[8,128]{1,0:T(8,128)}, f32[256,3072]{1,0:T(8,128)}) custom-call(bf16[4,384,768]{2,1,0:T(8,128)(2,1)S(1)} %get-tuple-element.9.h_ref, f32[8,128]{1,0:T(8,128)S(1)} %get-tuple-element.10.g_ref, f32[256,3072]{1,0:T(8,128)S(1)} %get-tuple-element.11.w_ref), custom_call_target="tpu_custom_call" | custom-call | tf_op jit(solution)/shard_map/pallas_call | solution.py:564

commit v5 on v4

--- a/solution.py
+++ b/solution.py
@@ -49,7 +49,6 @@
     barrier = pltpu.get_barrier_semaphore()
     for other in (side[0], side[1], to_xu, to_xd, to_yu, to_yd, sibling):
         pl.semaphore_signal(barrier, inc=1, device_id=other, device_id_type=MESH)
-    pl.semaphore_wait(barrier, 7)
 
     def ag(flow, t, j):
         owner = layer(-t) if flow == 0 else layer(t)
@@ -77,7 +76,6 @@
                 ag(flow, t - 1, j).wait_recv()
             ag(flow, t, j).start()
 
-    ag_step(0)
     cx = (c, y, x // 2, x % 2)
     own_tokens = pltpu.make_async_copy(og_ref, T.at[(*cx, slice(None), pl.ds(0, D))], loc.at[0])
     own_tokens.start()
@@ -111,6 +109,8 @@
     gates = jnp.dot(to_slot, weight.astype(BF), preferred_element_type=F32)
     T[c, y, x // 2, x % 2, :, D : D + EXPERTS] = ranks.astype(BF)
     T[c, y, x // 2, x % 2, :, D + EXPERTS : EXT] = jnp.transpose(gates).astype(BF)
+    pl.semaphore_wait(barrier, 7)
+    ag_step(0)
     own_tokens.wait()
 
     half = TOK // 2
@@ -261,12 +261,17 @@
             columns = slice(n * 128, (n + 1) * 128)
             S[l, :, columns] = (gate * H[l, :, columns].astype(F32)).astype(BF)
 
-    give_rows = remote(X.at[role[3]], Xf, ex_s.at[0], ex_r.at[0], partner)
+    def half_rows(a):
+        here = pl.ds(a * 16, 16)
+        return remote(X.at[role[3], :, here], Xf.at[:, here], ex_s.at[3 * a], ex_r.at[3 * a], partner)
+
+    give_rows = [half_rows(0), half_rows(1)]
     give_scaled = remote(S.at[role[3]], Sf, ex_s.at[1], ex_r.at[1], partner)
 
     pick_rows(role[3:], 0)
+    give_rows[0].start()
     pick_rows(role[3:], 1)
-    give_rows.start()
+    give_rows[1].start()
     scale(role[3])
     give_scaled.start()
     ag_step(3)
@@ -355,11 +360,11 @@
     term(2, reach(0, 4), Tm, 2)
     pl.semaphore_wait(free, 2)
     give_scaled.wait_recv()
-    give_rows.wait_recv()
+    for copy in give_rows:
+        copy.wait_recv()
     start(0)
+    ag_step(4)
     start(1)
-    ag_step(4)
-    start(2)
 
     def u_tile(rows, l, n):
         columns = pl.ds(pl.multiple_of(n * wide, wide), wide)
@@ -428,6 +433,7 @@
     SG[c, y, x] = jnp.zeros((NE, 128), F32)
 
     rs_step(1)
+    start(2)
     start(3)
     ag_step(5)
     rs_step(2)
@@ -488,7 +494,7 @@
     for t in range(6):
         for flow, t, j in ag_list(t):
             ag(flow, t, j).wait_send()
-    for copy in sends + [give_scaled, give_rows, give_u]:
+    for copy in sends + give_rows + [give_scaled, give_u]:
         copy.wait_send()
     for copies in slots:
         for copy in copies:
@@ -542,8 +548,8 @@
             dma((13,)),
             dma((7,)),
             dma((7,)),
-            dma((3,)),
-            dma((3,)),
+            dma((4,)),
+            dma((4,)),
             dma((12,)),
             pltpu.SemaphoreType.REGULAR,
         ],

time: 223 us -> 223 us (level)
  no operation moved by 1% of the time
where the time goes in v5:
time: 223 us; the launch traced here: 220 us
  Pallas kernels  219 us (98%)
    pallas_call x1, Pallas kernels, local(): pl.pallas_call(kernel, out_shape=(pltpu.VMEM((LOCAL, ROWS, HID), BF), plt...  217 us

profile of v5, /device:TPU:33, one launch (start us, length us, event | category | flops | bytes accessed | tf_op | source)
XLA Modules:
  0.0 220.1 jit_solution(1162480924448021299)
XLA Ops:
  0.6 216.9 %shard_map.85 = (bf16[4,384,768]{2,1,0:T(8,128)(2,1)S(1)}, f32[8,128]{1,0:T(8,128)S(1)}, f32[256,3072]{1,0:T(8,128)S(1)}) custom-call(bf16[256,3072]{1,0:T(8,128)(2,1)} %w_ref.1, bf16[128,2048]{1,0:T(8,128)(2,1)} %bitcast.23, s32[8,128]{1,0:T(8,128)} %bitcast.24, bf16[8,128]{1,0:T(8,128)(2,1)} %bitcast.26, s32[1,128]{1,0:T(1,128)} %bitcast.27, ...), custom_call_target="tpu_custom_call" | custom-call | flops 20000000000 | bytes 15000000 | tf_op jit(solution)/shard_map/pallas_call | solution.py:517
  217.5 2.5 %shard_map.86 = (bf16[4,384,768]{2,1,0:T(8,128)(2,1)}, f32[8,128]{1,0:T(8,128)}, f32[256,3072]{1,0:T(8,128)}) custom-call(bf16[4,384,768]{2,1,0:T(8,128)(2,1)S(1)} %get-tuple-element.9.h_ref, f32[8,128]{1,0:T(8,128)S(1)} %get-tuple-element.10.g_ref, f32[256,3072]{1,0:T(8,128)S(1)} %get-tuple-element.11.w_ref), custom_call_target="tpu_custom_call" | custom-call | tf_op jit(solution)/shard_map/pallas_call | solution.py:570
